TPU v7x, 32 devices: a whole 2x2x4 slice. The times are simulated.
32 devices in a mesh: comp: 4 (over z), sub: 8 (over y, x, core).
Axes of the slice: x: 2, y: 2, z: 4, core: 2. Of those that a mesh axis runs over, the one named last changes fastest.
Arguments:
- atmos_profiles: bfloat16 [4, 72, 262144], P(None, None, ('comp', 'sub')), may hold values from -6 to 6
- atmos_mixing: bfloat16 [72, 72], replicated
- drag_factor: float32 [262144], P(('comp', 'sub')), may hold values from 0.5 to 1.5
- surface_before: float32 [4, 262144], P(None, ('comp', 'sub')), may hold values from -6 to 6
- downward_fluxes: float32 [4, 262144], P(None, ('comp', 'sub')), may hold values from -6 to 6
- land_weight: float32 [262144], P(('comp', 'sub')), may hold values from 0.05 to 1
- land_surface: float32 [4, 262144], P(None, ('comp', 'sub')), may hold values from -6 to 6
- ocean_state: float32 [4, 60, 262144], P(None, None, ('comp', 'sub')), may hold values from -6 to 6
- ocean_mixing: float32 [60, 60], replicated
- sea_mask: int32 [262144], P(('comp', 'sub')), may hold values 0 or 1
- exchange_slot: int32 [4, 262144], P(None, ('comp', 'sub')), may hold values from 0 to 65535, as said below
- parent_column: int32 [4, 262144], P(None, ('comp', 'sub')), may hold values from 0 to 8191, as said below
- ocean_weight: float32 [4, 262144], P(None, ('comp', 'sub')), may hold values from 0.1 to 1
- atmos_weight: float32 [4, 262144], P(None, ('comp', 'sub')), may hold values from 0.05 to 0.5
Outputs:
- atmos_updated: bfloat16 [4, 72, 262144], P(None, None, ('comp', 'sub'))
- ocean_updated: float32 [4, 60, 262144], P(None, None, ('comp', 'sub'))
- surface_state: float32 [4, 262144], P(None, ('comp', 'sub'))
Inputs may be any that keep to these rules, and one draw needn't show every extreme that they name: Within the 8192 cells of one device block along the second dimension, all 32768 values are distinct, at most 2048 of them share one value of exchange_slot // 2048, and in every block some value of exchange_slot // 2048 is shared by exactly 2048 of them. In every aligned group of 128 cells along the second dimension (one k), the values are t * 128 + 0, 1, ..., 127 in order, for one t. In every aligned group of 128 cells along the second dimension (one k), all values share one value of parent_column // 128.
All inputs are finite; a program needn't handle non-finite values. No bound on the sum of `sea_mask` on one device may be relied on, other than what follows from the above.
Results may differ from a plain program's by a relative error of at most 0.001.
Values sent between devices are 32-bit elements; how exact they have to be, the bound alone decides.
No kernel may reach another device: no remote copies, remote signals or barrier semaphores. Data moves between devices by JAX's collectives and lax.ppermute only.
A program may use at most 128 MiB of HBM per device.

v0:
```python
import jax
import jax.numpy as jnp
from jax import lax
from jax.sharding import PartitionSpec as P

couple_rate = 0.5
highest = lax.Precision.HIGHEST


def surface_fluxes(atmos_profiles, drag_factor, surface_before, downward_fluxes):
    bottom = atmos_profiles[:, -1, :].astype(jnp.float32)
    east_gap = bottom[2] - surface_before[2]
    north_gap = bottom[3] - surface_before[3]
    wind_speed = jnp.sqrt(1.0 + east_gap * east_gap + north_gap * north_gap)
    transfer = drag_factor * wind_speed
    sensible = transfer * (surface_before[0] - bottom[0])
    latent = transfer * (surface_before[1] - bottom[1])
    return jnp.stack(
        [
            sensible,
            latent,
            transfer * east_gap,
            transfer * north_gap,
            downward_fluxes[0],
            downward_fluxes[1],
            downward_fluxes[2],
            downward_fluxes[3],
        ]
    )


def diffuse_atmos(atmos_profiles, atmos_mixing, fluxes):
    lowest = atmos_mixing[:, -1].astype(jnp.float32)
    tendency = couple_rate * jnp.stack([fluxes[0], fluxes[1], -fluxes[2], -fluxes[3]])
    result = []
    for member in range(4):
        mixed_rows = jnp.dot(
            atmos_mixing, atmos_profiles[member], preferred_element_type=jnp.float32
        )
        result.append(mixed_rows + lowest[:, None] * tendency[member][None, :])
    return jnp.stack(result).astype(jnp.bfloat16)


def forcing_rows(fluxes):
    return couple_rate * jnp.stack(
        [
            fluxes[4] + fluxes[5] - fluxes[0] - fluxes[1],
            fluxes[1] - fluxes[6] - fluxes[7],
            fluxes[2],
            fluxes[3],
        ]
    )


def per_device(
    atmos_profiles,
    atmos_mixing,
    drag_factor,
    surface_before,
    downward_fluxes,
    land_weight,
    land_surface,
    ocean_state,
    ocean_mixing,
    sea_mask,
    exchange_slot,
    parent_column,
    ocean_weight,
    atmos_weight,
):
    comp_count = lax.axis_size("comp")
    sub_count = lax.axis_size("sub")
    devices = comp_count * sub_count
    columns = atmos_profiles.shape[2]
    intersections = exchange_slot.shape[0]
    ocean_cells = exchange_slot.shape[1]
    capacity = 2 * intersections * ocean_cells // devices
    width = min(128, capacity)
    tile_count = intersections * ocean_cells // width
    slot_tiles = devices * capacity // width
    windows = columns // width
    tile_place = exchange_slot.reshape(tile_count, width)[:, 0] // width
    placement = (tile_place[None, :] == jnp.arange(slot_tiles, dtype=jnp.int32)[:, None]).astype(
        jnp.float32
    )

    def to_slots(values):
        return jnp.einsum("qt,ftl->fql", placement, values, precision=highest)

    wanted = parent_column.reshape(1, tile_count, width).astype(jnp.float32)
    request = (to_slots(wanted)[0] + 0.5).astype(jnp.int32).reshape(devices, capacity)
    asked_ids = lax.all_to_all(request, ("comp", "sub"), split_axis=0, concat_axis=0, tiled=True)
    asked_tiles = asked_ids.reshape(slot_tiles, width)
    window_hot = (
        (asked_tiles[:, 0] // width)[:, None] == jnp.arange(windows, dtype=jnp.int32)[None, :]
    ).astype(jnp.float32)
    lane_hot = (
        (asked_tiles % width)[:, :, None] == jnp.arange(width, dtype=jnp.int32)[None, None, :]
    ).astype(jnp.float32)
    fluxes = surface_fluxes(atmos_profiles, drag_factor, surface_before, downward_fluxes)
    column_forcing = forcing_rows(fluxes)
    window_rows = jnp.einsum(
        "qw,fwl->fql", window_hot, column_forcing.reshape(4, windows, width), precision=highest
    )
    served = jnp.einsum("fql,qml->fqm", window_rows, lane_hot, precision=highest)
    base_mix = jnp.stack(
        [jnp.dot(ocean_mixing, ocean_state[member], precision=highest) for member in range(4)]
    )
    arrived = lax.all_to_all(
        served.reshape(4, devices, capacity),
        ("comp", "sub"),
        split_axis=1,
        concat_axis=1,
        tiled=True,
    )
    atmos_updated = diffuse_atmos(atmos_profiles, atmos_mixing, fluxes)
    at_cells = jnp.einsum(
        "qt,fql->ftl", placement, arrived.reshape(4, slot_tiles, width), precision=highest
    ).reshape(4, intersections, ocean_cells)
    forcing = jnp.sum(ocean_weight[None] * at_cells, axis=1) / jnp.sum(ocean_weight, axis=0)[None]
    mixed_state = base_mix + ocean_mixing[:, 0][None, :, None] * forcing[:, None, :]
    ocean_updated = jnp.where(sea_mask[None, None, :] == 1, mixed_state, ocean_state)
    sea_share = atmos_weight * sea_mask.astype(jnp.float32)[None, :]
    outgoing = jnp.concatenate(
        [sea_share[None] * ocean_updated[:, 0, :][:, None, :], sea_share[None]], axis=0
    )
    send_buffer = to_slots(outgoing.reshape(5, tile_count, width))
    returned = lax.all_to_all(
        send_buffer.reshape(5, devices, capacity),
        ("comp", "sub"),
        split_axis=1,
        concat_axis=1,
        tiled=True,
    )
    lanes_back = jnp.einsum(
        "fqm,qml->fql", returned.reshape(5, slot_tiles, width), lane_hot, precision=highest
    )
    summed = jnp.einsum("qw,fql->fwl", window_hot, lanes_back, precision=highest).reshape(
        5, columns
    )
    surface_state = (summed[:4] + land_weight[None] * land_surface) / (summed[4] + land_weight)[
        None
    ]
    return (atmos_updated, ocean_updated, surface_state)


def solution(mesh):
    return jax.shard_map(
        per_device,
        mesh=mesh,
        in_specs=(
            P(None, None, ("comp", "sub")),
            P(),
            P(("comp", "sub")),
            P(None, ("comp", "sub")),
            P(None, ("comp", "sub")),
            P(("comp", "sub")),
            P(None, ("comp", "sub")),
            P(None, None, ("comp", "sub")),
            P(),
            P(("comp", "sub")),
            P(None, ("comp", "sub")),
            P(None, ("comp", "sub")),
            P(None, ("comp", "sub")),
            P(None, ("comp", "sub")),
        ),
        out_specs=(
            P(None, None, ("comp", "sub")),
            P(None, None, ("comp", "sub")),
            P(None, ("comp", "sub")),
        ),
        check_vma=False,
    )
```

profile of v0, /device:TPU:0, one launch (start us, length us, event | category | flops | bytes accessed | tf_op | source)
XLA Modules:
  0.0 196.8 jit_solution(3369608645898165822)
XLA Ops:
  0.7 1.0 reshape.161
  1.8 0.9 convert_element_type.43
  2.8 1.1 fusion.24
  3.9 7.3 %all-to-all-start = ((s32[32,1,2048]{2,1,0:T(1,128)}), s32[32,1,2048]{2,1,0:T(1,128)S(1)}, u32[]{:S(2)}, u32[]{:S(2)}) async-start(s32[32,1,2048]{2,1,0:T(1,128)} %bitcast.36), calls=%async_computation | async-start | bytes 524288 | tf_op jit(solution)/shard_map/all_to_all | solution.py:92
  11.2 1.1 slice_convert_fusion
  12.4 1.3 fusion.62
  15.2 6.6 %all-to-all-done = s32[32,1,2048]{2,1,0:T(1,128)S(1)} async-done(((s32[32,1,2048]{2,1,0:T(1,128)}), s32[32,1,2048]{2,1,0:T(1,128)S(1)}, u32[]{:S(2)}, u32[]{:S(2)}) %all-to-all-start) | async-done | bytes 262176 | tf_op jit(solution)/shard_map/all_to_all | solution.py:92
  23.2 32.7 %fusion.1 = f32[512,128,4]{1,2,0:T(4,128)} fusion(f32[4,512,128]{2,0,1:T(4,128)S(1)} %copy.74, s32[512,128]{1,0:T(8,128)S(1)} %add_select_fusion.1), kind=kOutput, calls=%fused_computation.2 | convolution fusion | flops 411041792 | bytes 2359296 | tf_op jit(solution)/shard_map/fql,qml->fqm/dot_general | solution.py:105
  55.9 2.8 %all-to-all-start.1 = ((f32[4,32,2048]{2,0,1:T(4,128)}), f32[4,32,2048]{2,0,1:T(4,128)S(1)}, u32[]{:S(2)}, u32[]{:S(2)}) async-start(f32[4,32,2048]{2,0,1:T(4,128)} %bitcast.48), calls=%async_computation.1 | async-start | bytes 2097152 | tf_op jit(solution)/shard_map/all_to_all | solution.py:109
  59.0 11.0 %copy.68 = f32[4,60,8192]{2,1,0:T(8,128)} copy(f32[4,60,8192]{2,0,1:T(4,128)} %param.21) | data formatting | bytes 15728640 | tf_op args[7]
  70.5 3.6 %convolution_bitcast_fusion = f32[1,60,8192]{2,1,0:T(8,128)S(1)} fusion(f32[60,60]{1,0:T(8,128)S(1)} %copy-done.2, f32[4,60,8192]{2,1,0:T(8,128)} %copy.68), kind=kOutput, calls=%fused_computation.9 | convolution fusion | flops 353894400 | bytes 4077632 | tf_op jit(solution)/shard_map/dot_general | solution.py:107
  74.2 4.8 %convolution_bitcast_fusion.1 = f32[1,60,8192]{2,1,0:T(8,128)} fusion(f32[60,60]{1,0:T(8,128)S(1)} %copy-done.2, f32[4,60,8192]{2,1,0:T(8,128)} %copy.68), kind=kOutput, calls=%fused_computation.10 | convolution fusion | flops 353894400 | bytes 4077632 | tf_op jit(solution)/shard_map/dot_general | solution.py:107
  79.0 3.2 %convolution_bitcast_fusion.2 = f32[1,60,8192]{2,1,0:T(8,128)} fusion(f32[60,60]{1,0:T(8,128)S(1)} %copy-done.2, f32[4,60,8192]{2,1,0:T(8,128)S(1)} %copy-done.1), kind=kOutput, calls=%fused_computation.11 | convolution fusion | flops 353894400 | bytes 4096000 | tf_op jit(solution)/shard_map/dot_general | solution.py:107
  82.2 3.5 %convolution_bitcast_fusion.3 = f32[1,60,8192]{2,1,0:T(8,128)} fusion(f32[60,60]{1,0:T(8,128)S(1)} %copy-done.2, f32[4,60,8192]{2,1,0:T(8,128)S(1)} %copy-done.1), kind=kOutput, calls=%fused_computation.12 | convolution fusion | flops 353894400 | bytes 4096000 | tf_op jit(solution)/shard_map/dot_general | solution.py:107
  86.5 1.6 copy.77
  88.1 1.4 reshape.164
  89.5 1.8 convolution_bitcast_fusion.6
  91.3 1.2 copy.79
  92.7 1.3 multiply_reduce_fusion
  94.1 9.4 %fusion.12 = f32[4,60,8192]{2,1,0:T(8,128)S(1)} fusion(f32[1,60,8192]{2,1,0:T(8,128)S(1)} %convolution_bitcast_fusion, f32[1,60,8192]{2,1,0:T(8,128)} %convolution_bitcast_fusion.1, f32[1,60,8192]{2,1,0:T(8,128)} %convolution_bitcast_fusion.2, f32[1,60,8192]{2,1,0:T(8,128)} %convolution_bitcast_fusion.3, f32[4,8192]{1,0:T(4,128)S(1)} %broadcast_divide_fusion, ...), kind=kLoop, calls=%fused_computation.22 | loop fusion | flops 11796480 | bytes 23732464 | tf_op jit(solution)/shard_map/jit(_where)/select_n | solution.py:122
  103.5 3.2 %copy-done = f32[4,60,8192]{2,1,0:T(8,128)} copy-done((f32[4,60,8192]{2,1,0:T(8,128)}, f32[4,60,8192]{2,1,0:T(8,128)S(1)}, u32[]{:S(2)}) %copy-start) | copy-done | bytes 7864344
  108.9 2.2 %copy.85 = f32[5,32,2048]{2,0,1:T(8,128)} copy(f32[5,32,2048]{2,1,0:T(8,128)S(1)} %reshape.166) | data formatting | bytes 2621440 | tf_op jit(solution)/shard_map/reshape | solution.py:129
  111.1 6.1 %all-to-all-start.2 = ((f32[5,32,2048]{2,0,1:T(8,128)}), f32[5,32,2048]{2,0,1:T(8,128)S(1)}, u32[]{:S(2)}, u32[]{:S(2)}) async-start(f32[5,32,2048]{2,0,1:T(8,128)} %copy.85), calls=%async_computation.2 | async-start | bytes 4194304 | tf_op jit(solution)/shard_map/all_to_all | solution.py:128
  117.5 1.7 fusion.10
  119.3 1.7 fusion.11
  121.0 1.7 fusion.8
  122.8 1.7 fusion.9
  124.5 2.5 %pad_maximum_fusion = bf16[4,72,8192]{2,1,0:T(8,128)(2,1)} fusion(bf16[1,72,8192]{2,1,0:T(8,128)(2,1)S(1)} %fusion.8, bf16[1,72,8192]{2,1,0:T(8,128)(2,1)S(1)} %fusion.9, bf16[1,72,8192]{2,1,0:T(8,128)(2,1)S(1)} %fusion.10, bf16[1,72,8192]{2,1,0:T(8,128)(2,1)S(1)} %fusion.11), kind=kLoop, calls=%fused_computation.23 | loop fusion | flops 7077888 | bytes 9437184 | tf_op jit(solution)/shard_map/stack | solution.py:41
  127.0 11.7 %copy.89 = f32[4,60,8192]{2,0,1:T(4,128)} copy(f32[4,60,8192]{2,1,0:T(8,128)} %copy-done) | data formatting | bytes 15728640
  138.7 27.3 %all-to-all-done.2 = f32[5,32,2048]{2,0,1:T(8,128)S(1)} async-done(((f32[5,32,2048]{2,0,1:T(8,128)}), f32[5,32,2048]{2,0,1:T(8,128)S(1)}, u32[]{:S(2)}, u32[]{:S(2)}) %all-to-all-start.2) | async-done | bytes 1310752 | tf_op jit(solution)/shard_map/all_to_all | solution.py:128
  166.0 29.3 %fusion.13 = f32[5,512,128]{2,0,1:T(8,128)S(1)} fusion(f32[5,512,128]{2,0,1:T(8,128)S(1)} %bitcast.141, s32[512,128]{1,0:T(8,128)S(1)} %copy-done.7), kind=kOutput, calls=%fused_computation.28 | convolution fusion | flops 511705088 | bytes 2883584 | tf_op jit(solution)/shard_map/fqm,qml->fql/dot_general | solution.py:135
  196.0 0.8 fusion.41
  (71 shorter events, 7.8 us)
Async XLA Ops:
  0.6 13.1 %copy-start.9 = (f32[4,8192]{1,0:T(4,128)S(1)}, f32[4,8192]{1,0:T(4,128)}, u32[]{:S(2)}) copy-start(f32[4,8192]{1,0:T(4,128)} %param.17) | copy-start | bytes 393220
  0.6 13.3 %copy-start.16 = (f32[8192]{0:T(1024)S(1)}, f32[8192]{0:T(1024)}, u32[]{:S(2)}) copy-start(f32[8192]{0:T(1024)} %param.16) | copy-start | bytes 98308
  0.7 13.9 %copy-start.11 = (s32[8192]{0:T(1024)S(1)}, s32[8192]{0:T(1024)}, u32[]{:S(2)}) copy-start(s32[8192]{0:T(1024)} %param.23) | copy-start | bytes 98308
  3.9 17.9 %all-to-all-start = ((s32[32,1,2048]{2,1,0:T(1,128)}), s32[32,1,2048]{2,1,0:T(1,128)S(1)}, u32[]{:S(2)}, u32[]{:S(2)}) async-start(s32[32,1,2048]{2,1,0:T(1,128)} %bitcast.36), calls=%async_computation | async-start | bytes 524288 | tf_op jit(solution)/shard_map/all_to_all | solution.py:92
  22.2 33.8 %copy-start.6 = (s32[512,128]{1,0:T(8,128)}, s32[512,128]{1,0:T(8,128)S(1)}, u32[]{:S(2)}) copy-start(s32[512,128]{1,0:T(8,128)S(1)} %add_select_fusion.1) | copy-start | bytes 786436
  23.2 35.6 %copy-start.12 = (f32[4,8192]{1,0:T(4,128)S(1)}, f32[4,8192]{1,0:T(4,128)}, u32[]{:S(2)}) copy-start(f32[4,8192]{1,0:T(4,128)} %param.27) | copy-start | bytes 393220
  55.9 30.6 %all-to-all-start.1 = ((f32[4,32,2048]{2,0,1:T(4,128)}), f32[4,32,2048]{2,0,1:T(4,128)S(1)}, u32[]{:S(2)}, u32[]{:S(2)}) async-start(f32[4,32,2048]{2,0,1:T(4,128)} %bitcast.48), calls=%async_computation.1 | async-start | bytes 2097152 | tf_op jit(solution)/shard_map/all_to_all | solution.py:109
  59.0 11.3 %copy-start.3 = (f32[4,8192]{1,0:T(4,128)S(1)}, f32[4,8192]{1,0:T(4,128)}, u32[]{:S(2)}) copy-start(f32[4,8192]{1,0:T(4,128)} %param.26) | copy-start | bytes 393220
  59.0 11.4 %copy-start.2 = (f32[60,60]{1,0:T(8,128)S(1)}, f32[60,60]{1,0:T(8,128)}, u32[]{:S(2)}) copy-start(f32[60,60]{1,0:T(8,128)} %param.22) | copy-start | bytes 43204
  70.5 8.4 %copy-start.1 = (f32[4,60,8192]{2,1,0:T(8,128)S(1)}, f32[4,60,8192]{2,1,0:T(8,128)}, u32[]{:S(2)}) copy-start(f32[4,60,8192]{2,1,0:T(8,128)} %copy.68) | copy-start | bytes 23592964
  82.2 3.5 %copy-start.13 = (f32[8192]{0:T(1024)S(1)}, f32[8192]{0:T(1024)}, u32[]{:S(2)}) copy-start(f32[8192]{0:T(1024)} %get-tuple-element.19) | copy-start | bytes 98308
  82.2 3.5 %copy-start.14 = (f32[8192]{0:T(1024)S(1)}, f32[8192]{0:T(1024)}, u32[]{:S(2)}) copy-start(f32[8192]{0:T(1024)} %get-tuple-element.34) | copy-start | bytes 98308
  82.2 3.5 %copy-start.15 = (f32[8192]{0:T(1024)S(1)}, f32[8192]{0:T(1024)}, u32[]{:S(2)}) copy-start(f32[8192]{0:T(1024)} %get-tuple-element.37) | copy-start | bytes 98308
  103.5 3.2 %copy-start = (f32[4,60,8192]{2,1,0:T(8,128)}, f32[4,60,8192]{2,1,0:T(8,128)S(1)}, u32[]{:S(2)}) copy-start(f32[4,60,8192]{2,1,0:T(8,128)S(1)} %fusion.12) | copy-start | bytes 23592964
  111.1 6.1 %copy-start.4 = (f32[4,8192]{1,0:T(4,128)S(1)}, f32[4,8192]{1,0:T(4,128)}, u32[]{:S(2)}) copy-start(f32[4,8192]{1,0:T(4,128)} %maximum_multiply_fusion) | copy-start | bytes 393220
  111.1 6.2 %copy-start.5 = (bf16[72,72]{1,0:T(8,128)(2,1)S(1)}, bf16[72,72]{1,0:T(8,128)(2,1)}, u32[]{:S(2)}) copy-start(bf16[72,72]{1,0:T(8,128)(2,1)} %param.15) | copy-start | bytes 31108
  111.1 54.9 %all-to-all-start.2 = ((f32[5,32,2048]{2,0,1:T(8,128)}), f32[5,32,2048]{2,0,1:T(8,128)S(1)}, u32[]{:S(2)}, u32[]{:S(2)}) async-start(f32[5,32,2048]{2,0,1:T(8,128)} %copy.85), calls=%async_computation.2 | async-start | bytes 4194304 | tf_op jit(solution)/shard_map/all_to_all | solution.py:128
  127.0 39.0 %copy-start.7 = (s32[512,128]{1,0:T(8,128)S(1)}, s32[512,128]{1,0:T(8,128)}, u32[]{:S(2)}) copy-start(s32[512,128]{1,0:T(8,128)} %copy-done.6) | copy-start | bytes 786436
  166.0 30.0 %copy-start.8 = (f32[8192]{0:T(1024)S(1)}, f32[8192]{0:T(1024)}, u32[]{:S(2)}) copy-start(f32[8192]{0:T(1024)} %param.19) | copy-start | bytes 98308
  166.0 30.0 %copy-start.10 = (f32[4,8192]{1,0:T(4,128)S(1)}, f32[4,8192]{1,0:T(4,128)}, u32[]{:S(2)}) copy-start(f32[4,8192]{1,0:T(4,128)} %param.20) | copy-start | bytes 393220
where the time goes:
time: 198 us; the launch traced here: 197 us
  matrix products  89.1 us (45%)
  local copies, waits for them, and re-layouts  36.2 us (18%)
  waiting for transfers between devices  33.9 us (17%)
  other arithmetic  20.3 us (10%)
  starting transfers between devices  16.2 us (8%)
    dot_general x1, matrix products, per_device(): jnp.einsum('fql,qml->fqm', window_rows, lane_hot, precision=highest)  32.7 us
    dot_general x1, matrix products, per_device(): jnp.einsum('fqm,qml->fql', returned.reshape(5, slot_tiles, width), lane_h...  29.3 us
    all_to_all x1, waiting for transfers between devices, per_device(): lax.all_to_all(send_buffer.reshape(5, devices, capacity), ('comp', 'sub')...  27.3 us
    unnamed x39, local copies, waits for them, and re-layouts  26.2 us
    dot_general x4, matrix products, per_device(): jnp.dot(ocean_mixing, ocean_state[member], precision=highest)  15.2 us
    select_n x1, other arithmetic, per_device(): jnp.where(sea_mask[None, None, :] == 1, mixed_state, ocean_state)  9.37 us
    all_to_all x1, starting transfers between devices, per_device(): lax.all_to_all(request, ('comp', 'sub'), split_axis=0, concat_axis=0, til...  7.3 us
    dot_general x4, matrix products, diffuse_atmos(): jnp.dot(atmos_mixing, atmos_profiles[member], preferred_element_type=jnp....  6.98 us
  transfers between devices with their start and end apart: 3, of which 2 were waited for; matrix products, arithmetic and copies ran while one was open for 27% of the time, Pallas kernels for 0%

commit v1 on v0

v1 whole, which is shorter than its diff:
```python
import functools

import jax
import jax.numpy as jnp
from jax import lax
from jax.experimental import pallas as pl
from jax.experimental.pallas import tpu as pltpu
from jax.sharding import PartitionSpec as P

couple_rate = 0.5
LANES = 128
VMEM_BYTES = 56 * 1024 * 1024
params = pltpu.CompilerParams(vmem_limit_bytes=VMEM_BYTES)
vmem = pl.BlockSpec(memory_space=pltpu.VMEM)
smem = pl.BlockSpec(memory_space=pltpu.SMEM)
AXES = ("comp", "sub")


def window(index):
    return pl.ds(pl.multiple_of(index * LANES, LANES), LANES)


def surface_rates(bottom, drag_factor, surface_before, downward):
    east = bottom[2] - surface_before[2]
    north = bottom[3] - surface_before[3]
    transfer = drag_factor * jnp.sqrt(1.0 + east * east + north * north)
    sensible = transfer * (surface_before[0] - bottom[0])
    latent = transfer * (surface_before[1] - bottom[1])
    east_stress = couple_rate * (transfer * east)
    north_stress = couple_rate * (transfer * north)
    forcing = jnp.stack(
        [
            couple_rate * (downward[0] + downward[1] - sensible - latent),
            couple_rate * (latent - downward[2] - downward[3]),
            east_stress,
            north_stress,
        ]
    )
    tendency = jnp.stack(
        [couple_rate * sensible, couple_rate * latent, -east_stress, -north_stress]
    )
    return forcing, tendency


def atmos_kernel(mix_ref, tend_ref, x_ref, out_ref):
    mix = mix_ref[...]
    lowest = mix[:, mix.shape[1] - 1 :].astype(jnp.float32)
    for member in range(x_ref.shape[0]):
        mixed = jnp.dot(mix, x_ref[member], preferred_element_type=jnp.float32)
        out_ref[member] = (mixed + lowest * tend_ref[member : member + 1, :]).astype(jnp.bfloat16)


def diffuse_atmos(profiles, mixing, tendency):
    fields, levels, columns = profiles.shape
    block = min(1024, columns)
    return pl.pallas_call(
        atmos_kernel,
        grid=(columns // block,),
        in_specs=[
            pl.BlockSpec((levels, levels), lambda i: (0, 0)),
            pl.BlockSpec((fields, block), lambda i: (0, i)),
            pl.BlockSpec((fields, levels, block), lambda i: (0, 0, i)),
        ],
        out_specs=pl.BlockSpec((fields, levels, block), lambda i: (0, 0, i)),
        out_shape=jax.ShapeDtypeStruct(profiles.shape, jnp.bfloat16),
        compiler_params=params,
        cost_estimate=pl.CostEstimate(
            flops=2 * fields * levels * levels * columns,
            bytes_accessed=4 * fields * levels * columns,
            transcendentals=0,
        ),
        name="diffuse_atmos",
    )(mixing, tendency, profiles)


def top_kernel(mix_ref, x_ref, out_ref):
    levels = x_ref.shape[0]
    total = mix_ref[0, 0] * x_ref[0]
    for level in range(1, levels):
        total = total + mix_ref[0, level] * x_ref[level]
    out_ref[...] = total


def top_level(state, mixing):
    levels, fields, cells = state.shape
    block = min(1024, cells)
    return pl.pallas_call(
        top_kernel,
        grid=(cells // block,),
        in_specs=[smem, pl.BlockSpec((levels, fields, block), lambda i: (0, 0, i))],
        out_specs=pl.BlockSpec((fields, block), lambda i: (0, i)),
        out_shape=jax.ShapeDtypeStruct((fields, cells), jnp.float32),
        compiler_params=params,
        cost_estimate=pl.CostEstimate(
            flops=2 * fields * levels * cells,
            bytes_accessed=4 * fields * levels * cells,
            transcendentals=0,
        ),
        name="top_level",
    )(mixing[0:1], state)


def scatter_lanes(values, lanes, column_ids):
    hot = jnp.where(column_ids == lanes, 1.0, 0.0).astype(jnp.bfloat16)
    high = values.astype(jnp.bfloat16).astype(jnp.float32)
    rows = values.shape[0]
    parts = jnp.concatenate([high, values - high], axis=0).astype(jnp.bfloat16)
    spread = lax.dot_general(
        parts, hot, (((1,), (1,)), ((), ())), preferred_element_type=jnp.float32
    )
    return spread[:rows] + spread[rows:]


def share_kernel(per_owner, place_ref, column_ref, weight_ref, mask_ref, wins_ref, out_ref):
    intersections, cells = column_ref.shape
    windows = cells // LANES
    out_ref[...] = jnp.zeros(out_ref.shape, jnp.float32)
    out_ref[:, :, per_owner * LANES :] = wins_ref[...]
    column_ids = lax.broadcasted_iota(jnp.int32, (LANES, LANES), 0)

    def body(spot, carry):
        mask = mask_ref[:, window(spot)].astype(jnp.float32)
        lanes = column_ref[:, window(spot)] & (LANES - 1)
        share = weight_ref[:, window(spot)] * mask
        for k in range(intersections):
            place = place_ref[k * windows + spot]
            row = jnp.broadcast_to(share[k : k + 1], (4, LANES))
            spread = scatter_lanes(row, lanes[k : k + 1], column_ids)
            out_ref[place // per_owner, :, window(place % per_owner)] = spread[0:1]
        return carry

    lax.fori_loop(0, windows, body, 0, unroll=2)


def middle_kernel(
    per_owner,
    place_ref,
    window_ref,
    corner_ref,
    gathered_ref,
    column_ref,
    ocean_weight_ref,
    atmos_weight_ref,
    mask_ref,
    base_ref,
    state_ref,
    forcing_ref,
    send_ref,
):
    intersections, cells = column_ref.shape
    windows = cells // LANES
    fields = base_ref.shape[0]
    send_ref[...] = jnp.zeros(send_ref.shape, jnp.float32)
    column_ids = lax.broadcasted_iota(jnp.int32, (LANES, LANES), 0)
    corner = corner_ref[0, 0]

    def body(spot, carry):
        here = window(spot)
        lanes = column_ref[:, here] & (LANES - 1)
        ocean_weight = ocean_weight_ref[:, here]
        total = jnp.zeros((fields, LANES), jnp.float32)
        weight = jnp.zeros((1, LANES), jnp.float32)
        for k in range(intersections):
            tile = k * windows + spot
            owner = place_ref[tile] // per_owner
            rows = gathered_ref[owner, :, window(window_ref[tile])]
            picked = jnp.take_along_axis(
                rows,
                jnp.broadcast_to(lanes[k : k + 1], (fields, LANES)),
                axis=1,
                mode="promise_in_bounds",
            )
            total = total + ocean_weight[k : k + 1] * picked
            weight = weight + ocean_weight[k : k + 1]
        forcing = total / weight
        forcing_ref[:, here] = forcing
        mask = mask_ref[:, here]
        surface = jnp.where(mask == 1, base_ref[:, here] + corner * forcing, state_ref[0, :, here])
        share = atmos_weight_ref[:, here] * mask.astype(jnp.float32)
        for k in range(intersections):
            place = place_ref[k * windows + spot]
            spread = scatter_lanes(share[k : k + 1] * surface, lanes[k : k + 1], column_ids)
            send_ref[place // per_owner, :, window(place % per_owner)] = spread
        return carry

    lax.fori_loop(0, windows, body, 0, unroll=2)


def ocean_kernel(fields, mix_ref, forcing_ref, mask_ref, x_ref, out_ref):
    levels, _, block = x_ref.shape
    x = x_ref[...]
    flat = x.reshape(levels * fields, block)
    row = lax.broadcasted_iota(jnp.int32, flat.shape, 0)
    push = jnp.concatenate(
        [forcing_ref[...], jnp.zeros((flat.shape[0] - fields, block), jnp.float32)], axis=0
    )
    loaded = flat + push
    high = loaded.astype(jnp.bfloat16)
    low = (loaded - high.astype(jnp.float32)).astype(jnp.bfloat16)
    mix = mix_ref[...]
    mix_high = mix.astype(jnp.bfloat16)
    mix_low = (mix - mix_high.astype(jnp.float32)).astype(jnp.bfloat16)
    mixed = (
        jnp.dot(mix_high, high, preferred_element_type=jnp.float32)
        + jnp.dot(mix_high, low, preferred_element_type=jnp.float32)
        + jnp.dot(mix_low, high, preferred_element_type=jnp.float32)
    )
    out_ref[...] = jnp.where(mask_ref[...] == 1, mixed, flat).reshape(levels, fields, block)


def diffuse_ocean(state, mixing, forcing, mask):
    levels, fields, cells = state.shape
    block = min(1024, cells)
    wide = jnp.kron(mixing, jnp.eye(fields, dtype=jnp.float32))
    return pl.pallas_call(
        functools.partial(ocean_kernel, fields),
        grid=(cells // block,),
        in_specs=[
            pl.BlockSpec(wide.shape, lambda i: (0, 0)),
            pl.BlockSpec((fields, block), lambda i: (0, i)),
            pl.BlockSpec((1, block), lambda i: (0, i)),
            pl.BlockSpec((levels, fields, block), lambda i: (0, 0, i)),
        ],
        out_specs=pl.BlockSpec((levels, fields, block), lambda i: (0, 0, i)),
        out_shape=jax.ShapeDtypeStruct(state.shape, jnp.float32),
        compiler_params=params,
        cost_estimate=pl.CostEstimate(
            flops=6 * (fields * levels) ** 2 * cells,
            bytes_accessed=8 * fields * levels * cells,
            transcendentals=0,
        ),
        name="diffuse_ocean",
    )(wide, forcing, mask, state)


def final_kernel(
    per_owner, wins_ref, share_ref, back_ref, land_weight_ref, land_ref, out_ref, *sums
):
    devices = back_ref.shape[0]
    for ref in sums:
        ref[...] = jnp.zeros(ref.shape, jnp.float32)
    chains = len(sums) // 2
    stride = devices // chains

    def body(step, carry):
        for slot in range(per_owner):
            for chain in range(chains):
                source = chain * stride + step
                spot = window(wins_ref[source * per_owner + slot])
                from_ = slice(slot * LANES, (slot + 1) * LANES)
                sums[chain][:, spot] += back_ref[source, :, from_]
                sums[chains + chain][:, spot] += share_ref[source, :, from_]
        return carry

    lax.fori_loop(0, stride, body, 0)
    total = land_weight_ref[...] * land_ref[...]
    weight = land_weight_ref[...]
    for chain in range(chains):
        total = total + sums[chain][...]
        weight = weight + sums[chains + chain][...]
    out_ref[...] = total / weight


def per_device(
    atmos_profiles,
    atmos_mixing,
    drag_factor,
    surface_before,
    downward_fluxes,
    land_weight,
    land_surface,
    ocean_state,
    ocean_mixing,
    sea_mask,
    exchange_slot,
    parent_column,
    ocean_weight,
    atmos_weight,
):
    devices = lax.axis_size("comp") * lax.axis_size("sub")
    fields, _, columns = atmos_profiles.shape
    intersections, cells = exchange_slot.shape
    capacity = 2 * intersections * cells // devices
    per_owner = capacity // LANES
    slots = devices * per_owner
    tiles = intersections * cells // LANES
    mask = sea_mask.reshape(1, cells)
    state = ocean_state.transpose(1, 0, 2)

    bottom = atmos_profiles[:, -1, :].astype(jnp.float32)
    forcing_rows, tendency = surface_rates(bottom, drag_factor, surface_before, downward_fluxes)
    gathered = lax.all_gather(forcing_rows, AXES, axis=0, tiled=False)

    place = exchange_slot.reshape(tiles, LANES)[:, 0] // LANES
    tile_window = parent_column.reshape(tiles, LANES)[:, 0] // LANES
    slot_window = jnp.sum(
        jnp.where(
            place[None, :] == jnp.arange(slots, dtype=jnp.int32)[:, None], tile_window[None, :], 0
        ),
        axis=1,
    )
    wins = jnp.pad(
        slot_window.astype(jnp.float32).reshape(devices, 1, per_owner),
        ((0, 0), (0, 0), (0, LANES - per_owner)),
    )
    share_send = pl.pallas_call(
        functools.partial(share_kernel, per_owner),
        in_specs=[smem, vmem, vmem, vmem, vmem],
        out_specs=vmem,
        out_shape=jax.ShapeDtypeStruct((devices, 1, (per_owner + 1) * LANES), jnp.float32),
        compiler_params=params,
        name="share_windows",
    )(place, parent_column, atmos_weight, mask, wins)
    share_back = lax.all_to_all(share_send, AXES, split_axis=0, concat_axis=0, tiled=True)
    back_windows = (
        share_back[:, 0, per_owner * LANES : per_owner * LANES + per_owner] + 0.5
    ).astype(jnp.int32).reshape(slots)

    atmos_updated = diffuse_atmos(atmos_profiles, atmos_mixing, tendency)
    base = top_level(state, ocean_mixing)

    forcing, send = pl.pallas_call(
        functools.partial(middle_kernel, per_owner),
        grid=(1,),
        in_specs=[
            smem,
            smem,
            smem,
            pl.BlockSpec((devices, fields, columns), lambda i: (0, 0, 0)),
            pl.BlockSpec((intersections, cells), lambda i: (0, 0)),
            pl.BlockSpec((intersections, cells), lambda i: (0, 0)),
            pl.BlockSpec((intersections, cells), lambda i: (0, 0)),
            pl.BlockSpec((1, cells), lambda i: (0, 0)),
            pl.BlockSpec((fields, cells), lambda i: (0, 0)),
            pl.BlockSpec((1, fields, cells), lambda i: (0, 0, 0)),
        ],
        out_specs=[
            pl.BlockSpec((fields, cells), lambda i: (0, 0)),
            pl.BlockSpec((devices, fields, capacity), lambda i: (0, 0, 0)),
        ],
        out_shape=[
            jax.ShapeDtypeStruct((fields, cells), jnp.float32),
            jax.ShapeDtypeStruct((devices, fields, capacity), jnp.float32),
        ],
        compiler_params=params,
        name="forcing_and_windows",
    )(
        place,
        tile_window,
        ocean_mixing[0:1, 0:1],
        gathered,
        parent_column,
        ocean_weight,
        atmos_weight,
        mask,
        base,
        state,
    )
    back = lax.all_to_all(send, AXES, split_axis=0, concat_axis=0, tiled=True)
    ocean_updated = diffuse_ocean(state, ocean_mixing, forcing, mask).transpose(1, 0, 2)

    chains = 4
    surface_state = pl.pallas_call(
        functools.partial(final_kernel, per_owner),
        in_specs=[smem, vmem, vmem, vmem, vmem],
        out_specs=vmem,
        out_shape=jax.ShapeDtypeStruct((fields, columns), jnp.float32),
        scratch_shapes=[pltpu.VMEM((fields, columns), jnp.float32)] * chains
        + [pltpu.VMEM((1, columns), jnp.float32)] * chains,
        compiler_params=params,
        name="surface_state",
    )(back_windows, share_back, back, land_weight.reshape(1, columns), land_surface)
    return (atmos_updated, ocean_updated, surface_state)


def solution(mesh):
    split = P(None, AXES)
    return jax.shard_map(
        per_device,
        mesh=mesh,
        in_specs=(
            P(None, None, AXES),
            P(),
            P(AXES),
            split,
            split,
            P(AXES),
            split,
            P(None, None, AXES),
            P(),
            P(AXES),
            split,
            split,
            split,
            split,
        ),
        out_specs=(P(None, None, AXES), P(None, None, AXES), split),
        check_vma=False,
    )
```

time: 198 us -> 140 us (0.71)
  matrix products: 89.1 us -> 0 us
  Pallas kernels: 0 us -> 53.1 us
  local copies, waits for them, and re-layouts: 36.2 us -> 14.9 us
  between operations: 1.13 us -> 14.1 us
  other arithmetic: 20.3 us -> 10.3 us
  starting transfers between devices: 16.2 us -> 10.5 us
    dot_general x15 -> x0, matrix products: 89.1 us -> none  [the longest x1 32.7 us: per_device(): jnp.einsum('fql,qml->fqm', window_rows, lane_hot, precision=highest)]
    pallas_call x0 -> x6, Pallas kernels: none -> 53.1 us  [the longest x1 14.6 us: per_device(): pl.pallas_call(functools.partial(middle_kernel, per_owner), grid=(1,), in...]
    all_gather x0 -> x1, waiting for transfers between devices: none -> 35.6 us  [per_device(): gathered = lax.all_gather(forcing_rows, AXES, axis=0, tiled=False)]
    all_to_all x3 -> x2, waiting for transfers between devices: 33.9 us -> 0.01 us  [the longest x1 0.01 us: per_device(): lax.all_to_all(share_send, AXES, split_axis=0, concat_axis=0, tiled=True)]
    unnamed x39 -> x12, local copies, waits for them, and re-layouts: 26.2 us -> 1.14 us
    select_n x4 -> x1, other arithmetic: 9.71 us -> 0.02 us  [per_device(): tile_window = parent_column.reshape(tiles, LANES)[:, 0] // LANES]
    mul x5 -> x1, local copies, waits for them, and re-layouts: 0.83 us -> 7.94 us  [diffuse_ocean(): wide = jnp.kron(mixing, jnp.eye(fields, dtype=jnp.float32))]
    all_to_all x3 -> x2, starting transfers between devices: 16.2 us -> 10.5 us  [the longest x1 7.3 us: per_device(): lax.all_to_all(share_send, AXES, split_axis=0, concat_axis=0, tiled=True)]
  transfers between devices with their start and end apart: 3 -> 3, of which waited for: 2 -> 1; matrix products, arithmetic and copies ran while one was open for 27% -> 14% of each run, Pallas kernels for 0% -> 36%
where the time goes in v1:
time: 140 us; the launch traced here: 139 us
  Pallas kernels  53.1 us (38%)
  waiting for transfers between devices  35.6 us (25%)
  local copies, waits for them, and re-layouts  14.9 us (11%)
  between operations  14.1 us (10%)
  starting transfers between devices  10.5 us (8%)
  other arithmetic  10.3 us (7%)
    all_gather x1, waiting for transfers between devices, per_device(): gathered = lax.all_gather(forcing_rows, AXES, axis=0, tiled=False)  35.6 us
    pallas_call x1, Pallas kernels, per_device(): pl.pallas_call(functools.partial(middle_kernel, per_owner), grid=(1,), in...  14.6 us
    pallas_call x1, Pallas kernels, diffuse_ocean(): pl.pallas_call(functools.partial(ocean_kernel, fields), grid=(cells // bl...  10.7 us
    pallas_call x1, Pallas kernels, per_device(): pl.pallas_call(functools.partial(share_kernel, per_owner), in_specs=[smem...  9.92 us
    mul x1, local copies, waits for them, and re-layouts, diffuse_ocean(): wide = jnp.kron(mixing, jnp.eye(fields, dtype=jnp.float32))  7.94 us
    pallas_call x1, Pallas kernels, diffuse_atmos(): pl.pallas_call(atmos_kernel, grid=(columns // block,), in_specs=[pl.Block...  7.89 us
    all_to_all x1, starting transfers between devices, per_device(): lax.all_to_all(share_send, AXES, split_axis=0, concat_axis=0, tiled=True)  7.3 us
    pallas_call x1, Pallas kernels, top_level(): pl.pallas_call(top_kernel, grid=(cells // block,), in_specs=[smem, pl.Blo...  6.82 us
  transfers between devices with their start and end apart: 3, of which 1 were waited for; matrix products, arithmetic and copies ran while one was open for 14% of the time, Pallas kernels for 36%

profile of v1, /device:TPU:0, one launch (start us, length us, event | category | flops | bytes accessed | tf_op | source)
XLA Modules:
  0.0 138.5 jit_solution(9287419421074065524)
XLA Ops:
  7.2 0.0 all-gather.4.cloned.1.call-start
  7.2 1.1 slice_convert_fusion
  8.4 1.3 fusion.9
  9.6 1.4 %fusion.3 = (f32[1,8192]{1,0:T(1,128)S(1)}, f32[1,8192]{1,0:T(1,128)S(1)}, f32[1,8192]{1,0:T(1,128)S(1)}, f32[1,8192]{1,0:T(1,128)S(1)}) fusion(f32[4,1,8192]{2,1,0:T(1,128)S(1)} %slice_convert_fusion, f32[4,8192]{1,0:T(4,128)} %param.17), kind=kLoop, calls=%fused_computation.13 | loop fusion | flops 32768 | bytes 393216 | tf_op jit(solution)/shard_map/sub | solution.py:24
  11.0 0.8 subtract_multiply_fusion.1
  11.9 0.8 maximum_bitcast_fusion
  12.6 0.0 all-gather.4.cloned.1.call-update
  12.7 1.0 reshape.115
  13.7 0.1 copy.26
  13.7 1.0 reshape.116
  14.8 0.1 copy.27
  14.9 0.1 select_reduce_fusion
  15.0 0.1 convert_element_type.36
  15.1 0.6 pad.4.wins_ref
  15.7 9.9 %share_windows.1 = f32[32,1,2176]{2,1,0:T(1,128)} custom-call(s32[256]{0:T(256)} %copy-done.3, s32[4,8192]{1,0:T(4,128)} %column_ref.3, f32[4,8192]{1,0:T(4,128)} %weight_ref.1, s32[1,8192]{1,0:T(1,128)} %bitcast.48, f32[32,1,128]{2,1,0:T(1,128)} %pad.4.wins_ref), custom_call_target="tpu_custom_call" | custom-call | tf_op jit(solution)/shard_map/share_windows/pallas_call | solution.py:306
  25.7 7.3 %all-to-all-start = ((f32[32,1,2176]{2,1,0:T(1,128)}), f32[32,1,2176]{2,1,0:T(1,128)S(1)}, u32[]{:S(2)}, u32[]{:S(2)}) async-start(f32[32,1,2176]{2,1,0:T(1,128)} %share_windows.1), calls=%async_computation | async-start | bytes 557056 | tf_op jit(solution)/shard_map/all_to_all | solution.py:314
  33.0 1.3 slice.86.mix_ref
  34.3 1.2 slice.81.corner_ref
  35.5 6.8 %top_level.1.base_ref = f32[4,8192]{1,0:T(4,128)} custom-call(f32[1,60]{1,0:T(1,128)} %slice.86.mix_ref, f32[60,4,8192]{2,1,0:T(4,128)} %bitcast.42), custom_call_target="tpu_custom_call" | custom-call | flops 3932160 | bytes 7864320 | tf_op jit(solution)/shard_map/top_level/pallas_call | solution.py:87
  42.3 35.6 %all-gather.4.cloned.1.call-done.gathered_ref = f32[32,4,8192]{2,1,0:T(4,128)} async-done(((f32[1,4,8192]{2,1,0:T(4,128)}), f32[32,4,8192]{2,1,0:T(4,128)}) %all-gather.4.cloned.1.call-update) | async-done | bytes 4194320 | tf_op jit(solution)/shard_map/all_gather | solution.py:292
  77.8 14.6 %forcing_and_windows.1 = (f32[4,8192]{1,0:T(4,128)}, f32[32,4,2048]{2,1,0:T(4,128)}) custom-call(s32[256]{0:T(256)} %copy-done.3, s32[256]{0:T(256)} %copy-done.4, f32[1,1]{1,0:T(1,128)} %slice.81.corner_ref, f32[32,4,8192]{2,1,0:T(4,128)} %all-gather.4.cloned.1.call-done.gathered_ref, s32[4,8192]{1,0:T(4,128)} %column_ref.3, f32[4,8192]{1,0:T(4,128)} %ocean_weight_ref.1, ...), custom_call_target="tpu_custom_call" | custom-call | tf_op jit(solution)/shard_map/forcing_and_windows/pallas_call | solution.py:322
  92.4 0.0 all-to-all-done.share_ref
  92.4 3.2 %all-to-all-start.1 = ((f32[32,4,2048]{2,1,0:T(4,128)}), f32[32,4,2048]{2,1,0:T(4,128)S(1)}, u32[]{:S(2)}, u32[]{:S(2)}) async-start(f32[32,4,2048]{2,1,0:T(4,128)} %get-tuple-element.6), calls=%async_computation.1 | async-start | bytes 2097152 | tf_op jit(solution)/shard_map/all_to_all | solution.py:359
  95.6 3.8 %broadcast_multiply_fusion = f32[60,4,60,4]{3,2,1,0:T(8,128)} fusion(f32[4,4]{1,0:T(4,128)S(1)} %fusion.6, f32[60,60]{1,0:T(8,128)S(1)} %copy-done.2), kind=kLoop, calls=%fused_computation | loop fusion | flops 57600 | bytes 244864 | tf_op jit(solution)/shard_map/jit(kron)/mul | solution.py:214
  99.4 7.9 %mul.77.mix_ref = f32[240,240]{1,0:T(8,128)} reshape(f32[60,4,60,4]{3,2,1,0:T(8,128)} %broadcast_multiply_fusion) | data formatting | bytes 460800 | tf_op jit(solution)/shard_map/jit(kron)/mul | solution.py:214
  107.3 0.8 pad_maximum_fusion.tend_ref
  108.1 7.9 %diffuse_atmos.1 = bf16[4,72,8192]{2,1,0:T(8,128)(2,1)} custom-call(bf16[72,72]{1,0:T(8,128)(2,1)} %mix_ref.1, f32[4,8192]{1,0:T(4,128)} %pad_maximum_fusion.tend_ref, bf16[4,72,8192]{2,1,0:T(8,128)(2,1)} %x_ref.1), custom_call_target="tpu_custom_call" | custom-call | flops 339738624 | bytes 9437184 | tf_op jit(solution)/shard_map/diffuse_atmos/pallas_call | solution.py:56
  116.0 0.1 fusion.5
  116.1 0.7 convert_element_type.38.wins_ref
  116.7 10.7 %diffuse_ocean.1 = f32[60,4,8192]{2,1,0:T(4,128)} custom-call(f32[240,240]{1,0:T(8,128)} %mul.77.mix_ref, f32[4,8192]{1,0:T(4,128)} %get-tuple-element.5.forcing_ref, s32[1,8192]{1,0:T(1,128)} %bitcast.50, f32[60,4,8192]{2,1,0:T(4,128)} %bitcast.44), custom_call_target="tpu_custom_call" | custom-call | flops 2831155200 | bytes 15728640 | tf_op jit(solution)/shard_map/diffuse_ocean/pallas_call | solution.py:215
  127.5 1.0 copy-done
  128.5 3.2 %surface_state.1 = f32[4,8192]{1,0:T(4,128)} custom-call(s32[512]{0:T(512)} %convert_element_type.38.wins_ref, f32[32,1,2176]{2,1,0:T(1,128)} %copy-done.1, f32[32,4,2048]{2,1,0:T(4,128)} %copy-done, f32[1,8192]{1,0:T(1,128)} %bitcast.71, f32[4,8192]{1,0:T(4,128)} %land_ref.1), custom_call_target="tpu_custom_call" | custom-call | tf_op jit(solution)/shard_map/surface_state/pallas_call | solution.py:363
  (14 shorter events, 0.1 us)
Async XLA Ops:
  7.2 70.7 %all-gather.4.cloned.1.call-start = ((), (), s32[]{:S(2)}) async-start(), calls=%async_computation.2 | async-start | bytes 4325376 | tf_op jit(solution)/shard_map/all_gather | solution.py:292
  14.9 0.9 copy-start.3
  14.9 63.0 %copy-start.4 = (s32[256]{0:T(256)}, s32[256]{0:T(256)S(1)}, u32[]{:S(2)}) copy-start(s32[256]{0:T(256)S(1)} %get-tuple-element.27.window_ref) | copy-start | bytes 3076
  25.7 66.7 %all-to-all-start = ((f32[32,1,2176]{2,1,0:T(1,128)}), f32[32,1,2176]{2,1,0:T(1,128)S(1)}, u32[]{:S(2)}, u32[]{:S(2)}) async-start(f32[32,1,2176]{2,1,0:T(1,128)} %share_windows.1), calls=%async_computation | async-start | bytes 557056 | tf_op jit(solution)/shard_map/all_to_all | solution.py:314
  42.3 53.3 %copy-start.2 = (f32[60,60]{1,0:T(8,128)S(1)}, f32[60,60]{1,0:T(8,128)}, u32[]{:S(2)}) copy-start(f32[60,60]{1,0:T(8,128)} %param.22) | copy-start | bytes 43204
  92.4 23.6 %copy-start.1 = (f32[32,1,2176]{2,1,0:T(1,128)}, f32[32,1,2176]{2,1,0:T(1,128)S(1)}, u32[]{:S(2)}) copy-start(f32[32,1,2176]{2,1,0:T(1,128)S(1)} %all-to-all-done.share_ref) | copy-start | bytes 835588
  92.4 35.1 %all-to-all-start.1 = ((f32[32,4,2048]{2,1,0:T(4,128)}), f32[32,4,2048]{2,1,0:T(4,128)S(1)}, u32[]{:S(2)}, u32[]{:S(2)}) async-start(f32[32,4,2048]{2,1,0:T(4,128)} %get-tuple-element.6), calls=%async_computation.1 | async-start | bytes 2097152 | tf_op jit(solution)/shard_map/all_to_all | solution.py:359
  127.5 1.0 copy-start
Sparse Core Ops, SparseCore 0:
  12.8 65.0 all-gather.3
